TPU v7x, 128 devices: a whole 4x4x4 slice. The times are simulated.
128 devices in a mesh: row: 8 (over y, core), col: 16 (over z, x).
Axes of the slice: x: 4, y: 4, z: 4, core: 2. Of those that a mesh axis runs over, the one named last changes fastest.
Arguments:
- lower_panel: float32 [7, 8, 2048, 4096], P(None, 'row', 'col'), may hold values from -0.0625 to 0.0625
- test_cross: float32 [7, 8, 2048, 1024], P(None, 'row', 'col'), may hold values from -6 to 6
- diag_inverse: float32 [2, 2048, 2048], P(None, 'col'), may hold values from -2 to 2, as said below
Outputs:
- solved: float32 [7, 8, 2048, 1024], P(None, 'row', 'col')
Inputs may be any that keep to these rules, and one draw needn't show every extreme that they name: `diag_inverse`: both matrices are lower triangular with a positive diagonal.
All inputs are finite; a program needn't handle non-finite values.
Results may differ from a plain program's by a relative error of at most 0.0001.
Values sent between devices are 32-bit elements; how exact they have to be, the bound alone decides.
A program may use at most 128 MiB of HBM per device.

v0:
```python
import jax
import jax.numpy as jnp
from jax import lax
from jax.sharding import PartitionSpec as P


def broadcast(array, axis, root):
    mine = lax.axis_index(axis) == root
    return lax.psum(jnp.where(mine, array, jnp.zeros_like(array)), axis)


def product(lower, solved_rows):
    return jnp.einsum(
        "arb,bt->art",
        lower,
        solved_rows,
        precision=lax.Precision.HIGHEST,
        preferred_element_type=jnp.float32,
    )


def on_device(lower_panel, test_cross, diag_inverse):
    blocks = lower_panel.shape[0]
    width = diag_inverse.shape[2]
    height = lax.axis_size("row")
    panel = lower_panel.reshape(blocks, lower_panel.shape[2], lower_panel.shape[3])
    current = test_cross.reshape(blocks, test_cross.shape[2], test_cross.shape[3])
    row_index = lax.axis_index("row")
    global_block = jnp.arange(blocks, dtype=jnp.int32) * height + row_index

    def solve_piece(step, rhs):
        part = diag_inverse[step]
        return jnp.dot(
            part,
            lax.all_gather(rhs, "col", axis=0, tiled=True),
            precision=lax.Precision.HIGHEST,
            preferred_element_type=jnp.float32,
        )

    def spread(piece, step):
        whole = lax.all_gather(piece, "col", axis=0, tiled=True)
        return broadcast(whole, "row", step)

    def update(state, lower, solved_rows, numbers, step):
        changed = state - product(lower, solved_rows)
        return jnp.where((numbers > step)[:, None, None], changed, state)

    first = solve_piece(0, current[0])
    first_full = spread(first, 0)
    current = update(current, panel[:, :, :width], first_full, global_block, 0)
    second = solve_piece(1, current[0])
    second_full = spread(second, 1)
    current = update(current, panel[:, :, width:], second_full, global_block, 1)
    leading = jnp.where(row_index == 0, first, jnp.where(row_index == 1, second, current[0]))
    current = jnp.concatenate([leading[None], current[1:]], axis=0)
    return current.reshape(test_cross.shape)


def solution(mesh):
    placed = (P(None, "row", "col", None), P(None, "row", "col", None), P(None, "col", None))
    return jax.shard_map(
        on_device,
        mesh=mesh,
        in_specs=placed,
        out_specs=P(None, "row", "col", None),
        check_vma=False,
    )
```

profile of v0, /device:TPU:1, one launch (start us, length us, event | category | flops | bytes accessed | tf_op | source)
XLA Modules:
  0.0 599.4 jit_solution(9589922194115427518)
XLA Ops:
  6.5 0.0 all-gather.11.cloned.1.call-start
  6.5 1.9 slice.26
  8.4 0.0 all-gather.11.cloned.1.call-update
  8.4 0.0 all-gather.7.cloned.1.call-start
  8.5 75.1 %all-gather.11.cloned.1.call-done = f32[1,1,2048,1024]{3,2,1,0:T(8,128)} async-done(((f32[1,1,128,1024]{3,2,1,0:T(8,128)}), f32[1,1,2048,1024]{3,2,1,0:T(8,128)}) %all-gather.11.cloned.1.call-update) | async-done | bytes 8388624 | tf_op jit(solution)/shard_map/all_gather | solution.py:35
  83.6 9.2 %fusion.6 = f32[128,1024]{1,0:T(8,128)} fusion(f32[1,1,2048,1024]{3,2,1,0:T(8,128)} %all-gather.11.cloned.1.call-done, f32[2,128,2048]{2,1,0:T(8,128)} %param.5), kind=kOutput, calls=%fused_computation.6 | convolution fusion | flops 3221225472 | bytes 9961472 | tf_op jit(solution)/shard_map/dot_general | solution.py:33
  92.8 0.0 all-gather.7.cloned.1.call-update
  92.8 0.0 all-reduce.3.cloned.1.call-start
  92.8 70.5 %all-gather.7.cloned.1.call-done = f32[2048,1024]{1,0:T(8,128)} async-done(((f32[128,1024]{1,0:T(8,128)}), f32[2048,1024]{1,0:T(8,128)}) %all-gather.7.cloned.1.call-update) | async-done | bytes 8388624 | tf_op jit(solution)/shard_map/all_gather | solution.py:41
  163.4 5.1 broadcast_select_fusion.1
  168.5 0.0 all-reduce.3.cloned.1.call-update
  168.5 0.0 all-gather.13.cloned.1.call-start
  168.6 104.2 %all-reduce.3.cloned.1.call-done = f32[2048,1024]{1,0:T(8,128)} async-done(((f32[2048,1024]{1,0:T(8,128)}), f32[2048,1024]{1,0:T(8,128)}) %all-reduce.3.cloned.1.call-update) | async-done | bytes 8388624 | tf_op jit(solution)/shard_map/psum | solution.py:9
  272.8 0.0 copy-start.2
  272.8 28.0 %subtract_select_fusion.1 = f32[7,128,1024]{2,1,0:T(8,128)S(1)} fusion(f32[7,1,128,1024]{3,2,1,0:T(8,128)} %param.4, f32[7,128,4096]{2,1,0:T(8,128)} %bitcast.47, f32[2048,1024]{1,0:T(8,128)} %all-reduce.3.cloned.1.call-done, pred[7]{0:T(512)(128)(4,1)S(1)} %fusion.29), kind=kOutput, calls=%fused_computation.11 | convolution fusion | flops 22550413312 | bytes 23068680 | tf_op jit(solution)/shard_map/arb,bt->art/dot_general | solution.py:13
  300.8 0.0 copy-start.3
  300.8 1.8 copy-done.3
  302.7 0.9 slice.34
  303.5 0.0 all-gather.13.cloned.1.call-update
  303.5 0.2 all-gather.9.cloned.1.call-start
  303.8 70.9 %all-gather.13.cloned.1.call-done = f32[1,2048,1024]{2,1,0:T(8,128)} async-done(((f32[1,128,1024]{2,1,0:T(8,128)}), f32[1,2048,1024]{2,1,0:T(8,128)}) %all-gather.13.cloned.1.call-update) | async-done | bytes 8388624 | tf_op jit(solution)/shard_map/all_gather | solution.py:35
  374.7 0.0 copy-done.2
  374.7 7.8 %fusion.18 = f32[128,1024]{1,0:T(8,128)} fusion(f32[1,2048,1024]{2,1,0:T(8,128)} %all-gather.13.cloned.1.call-done, f32[2,128,2048]{2,1,0:T(8,128)S(1)} %copy-done.2), kind=kOutput, calls=%fused_computation.15 | convolution fusion | flops 3221225472 | bytes 9961472 | tf_op jit(solution)/shard_map/dot_general | solution.py:33
  382.5 0.0 all-gather.9.cloned.1.call-update
  382.6 0.0 all-reduce.5.cloned.1.call-start
  382.6 70.5 %all-gather.9.cloned.1.call-done = f32[2048,1024]{1,0:T(8,128)} async-done(((f32[128,1024]{1,0:T(8,128)}), f32[2048,1024]{1,0:T(8,128)}) %all-gather.9.cloned.1.call-update) | async-done | bytes 8388624 | tf_op jit(solution)/shard_map/all_gather | solution.py:41
  453.1 8.5 %broadcast_select_fusion = f32[2048,1024]{1,0:T(8,128)} fusion(f32[2048,1024]{1,0:T(8,128)} %all-gather.9.cloned.1.call-done, pred[]{:T(512)S(6)} %eq.9), kind=kLoop, calls=%fused_computation.12 | loop fusion | flops 2097152 | bytes 16777216 | tf_op jit(solution)/shard_map/jit(_where)/select_n | solution.py:9
  461.7 0.0 all-reduce.5.cloned.1.call-update
  461.7 0.0 copy-start
  461.7 0.0 copy-start.1
  461.7 100.3 %all-reduce.5.cloned.1.call-done = f32[2048,1024]{1,0:T(8,128)} async-done(((f32[2048,1024]{1,0:T(8,128)}), f32[2048,1024]{1,0:T(8,128)}) %all-reduce.5.cloned.1.call-update) | async-done | bytes 8388624 | tf_op jit(solution)/shard_map/psum | solution.py:9
  562.0 27.9 %subtract_select_fusion = f32[7,128,1024]{2,1,0:T(8,128)S(1)} fusion(f32[7,128,1024]{2,1,0:T(8,128)} %copy-done.3, f32[7,128,4096]{2,1,0:T(8,128)} %bitcast.48, f32[2048,1024]{1,0:T(8,128)} %all-reduce.5.cloned.1.call-done, pred[7]{0:T(512)(128)(4,1)S(1)} %fusion.28), kind=kOutput, calls=%fused_computation.10 | convolution fusion | flops 22550413312 | bytes 23068680 | tf_op jit(solution)/shard_map/arb,bt->art/dot_general | solution.py:13
  589.9 0.0 copy-done
  589.9 0.0 copy-done.1
  589.9 0.1 fusion.27
  590.0 0.2 slice.37
  590.3 2.3 maximum_bitcast_fusion
  (2 shorter events, 0.0 us)
Async XLA Ops:
  6.5 77.1 %all-gather.11.cloned.1.call-start = ((), (), s32[]{:S(2)}) async-start(), calls=%async_computation.4 | async-start | bytes 8912896 | tf_op jit(solution)/shard_map/all_gather | solution.py:35
  8.4 154.9 %all-gather.7.cloned.1.call-start = ((), (), s32[]{:S(2)}) async-start(), calls=%async_computation | async-start | bytes 8912896 | tf_op jit(solution)/shard_map/all_gather | solution.py:41
  92.8 180.0 %all-reduce.3.cloned.1.call-start = ((), (), s32[]{:S(2)}) async-start(), calls=%async_computation.1 | async-start | bytes 16777216 | tf_op jit(solution)/shard_map/psum | solution.py:9
  168.5 206.2 %all-gather.13.cloned.1.call-start = ((), (), s32[]{:S(2)}) async-start(), calls=%async_computation.5 | async-start | bytes 8912896 | tf_op jit(solution)/shard_map/all_gather | solution.py:35
  272.8 101.9 %copy-start.2 = (f32[2,128,2048]{2,1,0:T(8,128)S(1)}, f32[2,128,2048]{2,1,0:T(8,128)}, u32[]{:S(2)}) copy-start(f32[2,128,2048]{2,1,0:T(8,128)} %param.5) | copy-start | bytes 6291460
  300.8 1.8 copy-start.3
  303.5 149.6 %all-gather.9.cloned.1.call-start = ((), (), s32[]{:S(2)}) async-start(), calls=%async_computation.2 | async-start | bytes 8912896 | tf_op jit(solution)/shard_map/all_gather | solution.py:41
  382.6 179.5 %all-reduce.5.cloned.1.call-start = ((), (), s32[]{:S(2)}) async-start(), calls=%async_computation.3 | async-start | bytes 16777216 | tf_op jit(solution)/shard_map/psum | solution.py:9
  461.7 128.2 %copy-start = (f32[128,1024]{1,0:T(8,128)S(1)}, f32[128,1024]{1,0:T(8,128)}, u32[]{:S(2)}) copy-start(f32[128,1024]{1,0:T(8,128)} %fusion.6) | copy-start | bytes 1572868
  461.7 128.2 %copy-start.1 = (f32[128,1024]{1,0:T(8,128)S(1)}, f32[128,1024]{1,0:T(8,128)}, u32[]{:S(2)}) copy-start(f32[128,1024]{1,0:T(8,128)} %fusion.18) | copy-start | bytes 1572868
Sparse Core Ops, SparseCore 0:
  9.5 74.0 all-gather.10
  92.9 70.4 all-gather.6
  168.7 104.0 all-reduce.2
  303.7 71.0 all-gather.12
  382.7 70.4 all-gather.8
  461.8 100.1 all-reduce.4
where the time goes:
time: 600 us; the launch traced here: 599 us
  waiting for transfers between devices  492 us (82%)
  matrix products  72.8 us (12%)
  other arithmetic  16.1 us (3%)
  between operations  13.6 us (2%)
    psum x2, waiting for transfers between devices, broadcast(): return lax.psum(jnp.where(mine, array, jnp.zeros_like(array)), axis)  205 us
    all_gather x2, waiting for transfers between devices, solve_piece(): lax.all_gather(rhs, 'col', axis=0, tiled=True)  146 us
    all_gather x2, waiting for transfers between devices, spread(): whole = lax.all_gather(piece, 'col', axis=0, tiled=True)  141 us
    dot_general x2, matrix products, product(): jnp.einsum('arb,bt->art', lower, solved_rows, precision=lax.Precision.HIG...  55.9 us
    dot_general x2, matrix products, solve_piece(): jnp.dot(part, lax.all_gather(rhs, 'col', axis=0, tiled=True), precision=l...  17 us
    select_n x2, other arithmetic, broadcast(): return lax.psum(jnp.where(mine, array, jnp.zeros_like(array)), axis)  13.7 us
  transfers between devices with their start and end apart: 6, of which 6 were waited for; matrix products, arithmetic and copies ran while one was open for 0% of the time, Pallas kernels for 0%

commit v1 on v0

v1 whole, which is shorter than its diff:
```python
import functools

import jax
import jax.numpy as jnp
from jax import lax
from jax.experimental import pallas as pl
from jax.experimental.pallas import tpu as pltpu
from jax.sharding import PartitionSpec as P

MESH = pl.DeviceIdType.MESH
DMA = pltpu.SemaphoreType.DMA
F32 = jnp.float32
BF16 = jnp.bfloat16
NEAR = 48


def split(value):
    high = value.astype(BF16)
    return high, (value - high.astype(F32)).astype(BF16)


def dot3(a, b):
    def dot(u, v):
        return jnp.dot(u, v, preferred_element_type=F32)

    return dot(a[0], b[0]) + (dot(a[0], b[1]) + dot(a[1], b[0]))


def kernel(
    panel, cross, diag, out,
    acc, lhi, llo, stage, dbuf, l10, b0, b1, b1_tile, ybuf, yhi, ylo,
    load_sem, stage_sem, out_sem,
    s_ss, s_rs, l_ss, l_rs, pg_ss, pg_rs, yt_ss, yt_rs, yd_ss, yd_rs, cc_ss, cc_rs,
):
    row, col = lax.axis_index("row"), lax.axis_index("col")
    y, core = lax.div(row, 2), lax.rem(row, 2)
    z, x = lax.div(col, 4), lax.rem(col, 4)

    def at(dy=0, dz=0, dx=0, other=False):
        c = 1 - core if other else core
        return (lax.rem(y + dy, 4) * 2 + c, lax.rem(z + dz, 4) * 4 + lax.rem(x + dx, 4))

    def send(src, dst, ss, rs, device):
        return pltpu.make_async_remote_copy(
            src_ref=src, dst_ref=dst, send_sem=ss, recv_sem=rs, device_id=device, device_id_type=MESH
        )

    sent = []

    def go(copy):
        copy.start()
        sent.append(copy)
        return copy

    barrier = pltpu.get_barrier_semaphore()
    partners = [at(dx=i) for i in (1, 2, 3)] + [at(dz=i) for i in (1, 2, 3)]
    partners += [at(dy=i, other=o) for i in range(4) for o in (False, True) if i or o]
    for device in partners:
        pl.semaphore_signal(barrier, inc=1, device_id=device, device_id_type=MESH)

    d_load = pltpu.make_async_copy(diag, dbuf, load_sem.at[0])
    d_load.start()
    l_loads = [
        pltpu.make_async_copy(panel.at[a, 0], stage.at[a % 2], stage_sem.at[a % 2]) for a in range(7)
    ]
    l_loads[0].start()
    l_loads[1].start()
    acc_loads = []
    for q in range(4):
        load = pltpu.make_async_copy(
            cross.at[:, 0, :, pl.ds(256 * q, 256)], acc.at[q], load_sem.at[1 + q]
        )
        load.start()
        acc_loads.append(load)

    def convert(a):
        l_loads[a].wait()
        high, low = split(stage[a % 2])
        lhi[a], llo[a] = high, low
        if a + 2 < 7:
            l_loads[a + 2].start()

    for a in range(3):
        convert(a)
    pl.semaphore_wait(barrier, len(partners))

    def tile_of(r):
        return cross.at[0, 0, :, pl.ds(128 * r, 128)]

    def b0_send(r):
        return send(tile_of(r), b0.at[z, x], s_ss.at[r], s_rs.at[0], (r, col))

    def b1_send(r):
        return send(tile_of(r), b1_tile, s_ss.at[r], s_rs.at[1], (r, col))

    def l10_half(h):
        return panel.at[0, 0, :, pl.ds(1024 * h, 1024)]

    def l10_send(r, h):
        return send(l10_half(h), l10.at[h], l_ss.at[r, h], l_rs.at[h], (r, col))

    l10_parts = [(0, 0), (0, 1)] + [(r, r % 2) for r in range(2, 8)]

    @pl.when(row == 0)
    def _():
        for r in (4, 5, 2, 3, 6, 7, 1):
            b0_send(r).start()
        pltpu.make_async_copy(tile_of(0), b0.at[z, x], s_rs.at[0]).start()

    @pl.when(row == 1)
    def _():
        for r in (4, 5, 2, 3, 6, 7, 0):
            b1_send(r).start()
        pltpu.make_async_copy(tile_of(1), b1_tile, s_rs.at[1]).start()
        for r, h in l10_parts:
            l10_send(r, h).start()
        for h in range(2):
            pltpu.make_async_copy(l10_half(h), l10.at[h], l_rs.at[h]).start()

    for a in range(3, 7):
        convert(a)

    class Gather:
        def __init__(self, number, view, lo, hi):
            self.number, self.view = number, view
            mid = (lo + hi) // 2
            self.first, self.second = pl.ds(lo, mid - lo), pl.ds(mid, hi - mid)

        def copy(self, kind, i, piece, device):
            return send(
                piece, piece, pg_ss.at[self.number, kind, i - 1], pg_rs.at[self.number, kind, i - 1], device
            )

        def phase1(self):
            self.one = []
            for i in (2, 1, 3):
                self.one.append(go(self.copy(0, i, self.view.at[z, x, self.first], at(dx=i))))
                self.one.append(go(self.copy(1, i, self.view.at[z, x, self.second], at(dz=i))))

        def phase2(self):
            for c in self.one:
                c.wait_recv()
            self.two = []
            for i in (2, 1, 3):
                self.two.append(go(self.copy(2, i, self.view.at[z, :, self.first], at(dz=i))))
                self.two.append(go(self.copy(3, i, self.view.at[:, x, self.second], at(dx=i))))

        def done(self):
            for c in self.two:
                c.wait_recv()

    def y_tiles(t):
        copies = {}
        for e in (2, 1, 3):
            rows = pl.ds(0, 128 if e == 2 else NEAR)
            piece = ybuf.at[t, row, z, x, rows]
            copies[e] = go(send(piece, piece, yt_ss.at[t, e - 1], yt_rs.at[t, e - 1], at(dy=e)))
        return copies

    def y_direct(t):
        copies = {}
        for e in (1, 3):
            piece = ybuf.at[t, row, :, :, pl.ds(NEAR, 128 - NEAR)]
            copies[e] = go(send(piece, piece, yd_ss.at[t, e // 2], yd_rs.at[t, e // 2], at(dy=e)))
        return copies

    def slice_of(d):
        return lax.rem(y + d, 4) * 2 + core

    def across(t, d):
        piece = ybuf.at[t, slice_of(d)]
        return go(send(piece, piece, cc_ss.at[t, d], cc_rs.at[t, d], at(other=True)))

    def own_gather(t):
        return Gather(2 + t, ybuf.at[t, row], 0, 128)

    def foreign(t):
        return {
            d: Gather(4 + 3 * t + d - 1, ybuf.at[t, slice_of(d)], 0, 128 if d == 2 else NEAR)
            for d in (2, 1, 3)
        }

    def update(t, d):
        q = lax.rem(y + d, 4)
        for half in range(2):
            high, low = split(ybuf[t, 2 * q + half].reshape(2048, 128))
            yhi[:, 128 * half : 128 * half + 128] = high
            ylo[:, 128 * half : 128 * half + 128] = low

        def body(a, carry):
            ks = slice(2048 * t, 2048 * t + 2048)
            acc[q, a] -= dot3((lhi[a, :, ks], llo[a, :, ks]), (yhi[...], ylo[...]))
            return carry

        lax.fori_loop(0, 7, body, 0)

    d_load.wait()
    send(b0.at[z, x], b0.at[z, x], s_ss.at[0], s_rs.at[0], (row, col)).wait_recv()
    g_b = Gather(0, b0, 0, 128)
    g_b.phase1()
    d0 = split(dbuf[0])
    g_b.phase2()

    l10_across = send(
        l10.at[core], l10.at[core], l_ss.at[1, 0], l_rs.at[core], at(other=True)
    )

    @pl.when(y > 0)
    def _():
        l10_across.wait_recv()
        l10_across.start()

    g_b.done()
    ybuf[0, row, z, x] = dot3(d0, split(b0[...].reshape(2048, 128)))
    own0 = own_gather(0)
    own0.phase1()
    tiles0 = y_tiles(0)
    own0.phase2()

    @pl.when(y > 0)
    def _():
        send(l10.at[core], l10.at[1 - core], l_ss.at[1, 0], l_rs.at[1 - core], at(other=True)).wait_recv()

    @pl.when(y == 0)
    def _():
        for h in range(2):
            send(l10.at[h], l10.at[h], l_ss.at[1, 0], l_rs.at[h], at(other=True)).wait_recv()

    send(b1_tile, b1_tile, s_ss.at[0], s_rs.at[1], (row, col)).wait_recv()
    own0.done()

    mine = ybuf[0, row].reshape(2048, 128)
    b1[z, x] = b1_tile[...] - (
        dot3(split(l10[0]), split(mine[:1024])) + dot3(split(l10[1]), split(mine[1024:]))
    )
    g_f = Gather(1, b1, 0, 128)
    g_f.phase1()
    cross0 = {0: across(0, 0)}
    direct0 = y_direct(0)
    g_f.phase2()
    far0 = foreign(0)
    for d in (2, 1, 3):
        tiles0[4 - d].wait_recv()
        far0[d].phase1()
    for load in acc_loads:
        load.wait()
    cross0[0].wait_recv()
    update(0, 0)
    g_f.done()
    ybuf[1, row, z, x] = dot3(split(dbuf[1]), split(b1[...].reshape(2048, 128)))
    own1 = own_gather(1)
    own1.phase1()
    tiles1 = y_tiles(1)
    for d in (2, 1, 3):
        far0[d].phase2()
    own1.phase2()
    far1 = foreign(1)
    for d in (2, 1, 3):
        tiles1[4 - d].wait_recv()
        far1[d].phase1()
    far0[2].done()
    cross0[2] = across(0, 2)
    for d in (1, 3):
        far0[d].done()
        direct0[4 - d].wait_recv()
        cross0[d] = across(0, d)
    own1.done()
    cross1 = {0: across(1, 0)}
    direct1 = y_direct(1)
    for d in (2, 1, 3):
        far1[d].phase2()
    for d in (2, 1, 3):
        cross0[d].wait_recv()
        update(0, d)

    def store(q):
        return pltpu.make_async_copy(
            acc.at[q], out.at[:, 0, :, pl.ds(pl.multiple_of(256 * q, 256), 256)], out_sem.at[q]
        )

    def finish(d):
        update(1, d)
        q = lax.rem(y + d, 4)

        @pl.when(row < 2)
        def _():
            for half in range(2):
                acc[q, 0, :, 128 * half : 128 * half + 128] = ybuf[row, 2 * q + half, z, x]

        store(q).start()

    cross1[0].wait_recv()
    finish(0)
    far1[2].done()
    cross1[2] = across(1, 2)
    for d in (1, 3):
        far1[d].done()
        direct1[4 - d].wait_recv()
        cross1[d] = across(1, d)
    for d in (2, 1, 3):
        cross1[d].wait_recv()
        finish(d)

    for c in sent:
        c.wait_send()

    @pl.when(row == 0)
    def _():
        for r in range(1, 8):
            b0_send(r).wait_send()

    @pl.when(row == 1)
    def _():
        for r in (0, 2, 3, 4, 5, 6, 7):
            b1_send(r).wait_send()
        for r, h in l10_parts:
            l10_send(r, h).wait_send()

    @pl.when(y > 0)
    def _():
        l10_across.wait_send()

    for q in range(4):
        store(q).wait()


def on_device(lower_panel, test_cross, diag_inverse):
    V = pltpu.VMEM
    return pl.pallas_call(
        kernel,
        out_shape=jax.ShapeDtypeStruct(test_cross.shape, F32),
        in_specs=[pl.BlockSpec(memory_space=pl.ANY)] * 3,
        out_specs=pl.BlockSpec(memory_space=pl.ANY),
        scratch_shapes=[
            V((4, 7, 128, 256), F32),
            V((7, 128, 4096), BF16),
            V((7, 128, 4096), BF16),
            V((2, 128, 4096), F32),
            V((2, 128, 2048), F32),
            V((2, 128, 1024), F32),
            V((4, 4, 128, 128), F32),
            V((4, 4, 128, 128), F32),
            V((128, 128), F32),
            V((2, 8, 4, 4, 128, 128), F32),
            V((2048, 256), BF16),
            V((2048, 256), BF16),
            DMA((5,)), DMA((2,)), DMA((4,)),
            DMA((8,)), DMA((2,)), DMA((8, 2)), DMA((2,)),
            DMA((10, 4, 3)), DMA((10, 4, 3)),
            DMA((2, 3)), DMA((2, 3)), DMA((2, 2)), DMA((2, 2)), DMA((2, 4)), DMA((2, 4)),
        ],
        compiler_params=pltpu.CompilerParams(
            collective_id=0, has_side_effects=True, vmem_limit_bytes=60 * 2**20
        ),
        cost_estimate=pl.CostEstimate(flops=22 * 10**9, bytes_accessed=24 * 10**6, transcendentals=0),
    )(lower_panel, test_cross, diag_inverse)


def solution(mesh):
    placed = (P(None, "row", "col", None), P(None, "row", "col", None), P(None, "col", None))
    return jax.shard_map(
        on_device,
        mesh=mesh,
        in_specs=placed,
        out_specs=P(None, "row", "col", None),
        check_vma=False,
    )
```

time: 600 us -> 123 us (0.20)
  the two profiles are of different devices: /device:TPU:1 before, /device:TPU:16 now
where the time goes in v1:
time: 123 us
  Pallas kernels  119 us (97%)
  local copies, waits for them, and re-layouts  4.37 us (4%)
    pallas_call x1, Pallas kernels, on_device(): pl.pallas_call(kernel, out_shape=jax.ShapeDtypeStruct(test_cross.shape, F...  119 us
    unnamed x1, local copies, waits for them, and re-layouts  4.37 us

profile of v1, /device:TPU:16, one launch (start us, length us, event | category | flops | bytes accessed | tf_op | source)
XLA Modules:
  0.0 123.1 jit_solution(2616888748759955085)
XLA Ops:
  0.0 118.7 %shard_map.37 = f32[7,1,128,1024]{3,2,1,0:T(8,128)} custom-call(f32[7,1,128,4096]{3,2,1,0:T(8,128)} %panel.1, f32[7,1,128,1024]{3,2,1,0:T(8,128)} %cross.1, f32[2,128,2048]{2,1,0:T(8,128)} %diag.1), custom_call_target="tpu_custom_call" | custom-call | flops 22000001024 | bytes 24000000 | tf_op jit(solution)/shard_map/pallas_call | solution.py:329
  118.7 4.4 %copy.5 = f32[7,1,128,1024]{3,2,1,0:T(8,128)} copy(f32[7,1,128,1024]{3,2,1,0:T(8,128)} %shard_map.37) | data formatting | bytes 7340032

commit v2 on v1

v2 whole, which is shorter than its diff:
```python
import jax
import jax.numpy as jnp
from jax import lax
from jax.experimental import pallas as pl
from jax.experimental.pallas import tpu as pltpu
from jax.sharding import PartitionSpec as P

MESH = pl.DeviceIdType.MESH
DMA = pltpu.SemaphoreType.DMA
F32 = jnp.float32
BF16 = jnp.bfloat16
NEAR = (0, 64)


def split(value):
    high = value.astype(BF16)
    return high, (value - high.astype(F32)).astype(BF16)


def dot3(a, b):
    def dot(u, v):
        return jnp.dot(u, v, preferred_element_type=F32)

    return dot(a[0], b[0]) + (dot(a[0], b[1]) + dot(a[1], b[0]))


def kernel(
    panel, cross, diag, out,
    lhi, llo, stage, dbuf, l10, b0, b1, b1_tile, ybuf, yhi, ylo,
    load_sem, stage_sem,
    s_ss, s_rs, l_ss, l_rs, pg_ss, pg_rs, yt_ss, yt_rs, yd_ss, yd_rs, yr_ss, yr_rs, cc_ss, cc_rs,
):
    row, col = lax.axis_index("row"), lax.axis_index("col")
    y, core = lax.div(row, 2), lax.rem(row, 2)
    z, x = lax.div(col, 4), lax.rem(col, 4)

    def at(dy=0, dz=0, dx=0, other=False):
        c = 1 - core if other else core
        return (lax.rem(y + dy, 4) * 2 + c, lax.rem(z + dz, 4) * 4 + lax.rem(x + dx, 4))

    def send(src, dst, ss, rs, device):
        return pltpu.make_async_remote_copy(
            src_ref=src, dst_ref=dst, send_sem=ss, recv_sem=rs, device_id=device, device_id_type=MESH
        )

    sent = []

    def go(make):
        make().start()
        sent.append(make)
        return make

    barrier = pltpu.get_barrier_semaphore()
    partners = [at(dx=i) for i in (1, 2, 3)] + [at(dz=i) for i in (1, 2, 3)]
    partners += [at(dy=i, other=o) for i in range(4) for o in (False, True) if i or o]
    for device in partners:
        pl.semaphore_signal(barrier, inc=1, device_id=device, device_id_type=MESH)

    d_load = pltpu.make_async_copy(diag, dbuf, load_sem.at[0])
    d_load.start()
    l_loads = [
        pltpu.make_async_copy(panel.at[a, 0], stage.at[a % 2], stage_sem.at[a % 2]) for a in range(7)
    ]
    l_loads[0].start()
    l_loads[1].start()
    out_load = pltpu.make_async_copy(cross, out, load_sem.at[1])
    out_load.start()

    def convert(a):
        l_loads[a].wait()

        def some_rows(g, carry):
            rows = pl.ds(pl.multiple_of(16 * g, 16), 16)
            to = pl.ds(pl.multiple_of(128 * a + 16 * g, 16), 16)
            left = lax.broadcasted_iota(jnp.int32, (16, 128), 1) < 64
            for t in range(2):
                for p in range(8):
                    one = stage[a % 2, rows, 2048 * t + 256 * p : 2048 * t + 256 * p + 128]
                    two = stage[a % 2, rows, 2048 * t + 256 * p + 128 : 2048 * t + 256 * p + 256]
                    parts = (
                        jnp.where(left, one, pltpu.roll(two, 64, 1)),
                        jnp.where(left, pltpu.roll(one, 64, 1), two),
                    )
                    for h in range(2):
                        high, low = split(parts[h])
                        lhi[t, h, to, 128 * p : 128 * p + 128] = high
                        llo[t, h, to, 128 * p : 128 * p + 128] = low
            return carry

        lax.fori_loop(0, 8, some_rows, 0)
        if a + 2 < 7:
            l_loads[a + 2].start()

    for a in range(2):
        convert(a)
    pl.semaphore_wait(barrier, len(partners))

    def tile_of(r):
        return cross.at[pl.ds(0, 128), pl.ds(128 * r, 128)]

    def b0_send(r):
        return send(tile_of(r), b0.at[z, x], s_ss.at[r], s_rs.at[0], (r, col))

    def b1_send(r):
        return send(tile_of(r), b1_tile, s_ss.at[r], s_rs.at[1], (r, col))

    def l10_half(h):
        return panel.at[0, 0, :, pl.ds(1024 * h, 1024)]

    def l10_send(r, h):
        return send(l10_half(h), l10.at[h], l_ss.at[r, h], l_rs.at[h], (r, col))

    l10_parts = [(2, 0), (7, 1), (3, 1), (6, 0), (0, 0), (0, 1)]

    @pl.when(row == 0)
    def _():
        for r in (4, 5, 2, 3, 6, 7, 1):
            b0_send(r).start()
        pltpu.make_async_copy(tile_of(0), b0.at[z, x], s_rs.at[0]).start()

    for a in range(2, 5):
        convert(a)

    @pl.when(row == 1)
    def _():
        for r, h in l10_parts[:4]:
            l10_send(r, h).start()
        for r in (4, 5, 2, 3, 6, 7, 0):
            b1_send(r).start()
        pltpu.make_async_copy(tile_of(1), b1_tile, s_rs.at[1]).start()
        for r, h in l10_parts[4:]:
            l10_send(r, h).start()
        for h in range(2):
            pltpu.make_async_copy(l10_half(h), l10.at[h], l_rs.at[h]).start()

    for a in range(5, 7):
        convert(a)

    class Gather:
        def __init__(self, number, view, lo, hi):
            self.number, self.view = number, view
            mid = (lo + hi) // 2
            self.rows = (lo, mid - lo), (mid, hi - mid)

        def tile(self, half, dz=0, dx=0):
            return self.view.at[lax.rem(z + dz, 4), lax.rem(x + dx, 4), pl.ds(*self.rows[half])]

        def line(self, half):
            if half == 0:
                return self.view.at[z, :, pl.ds(*self.rows[half])]
            return self.view.at[:, x, pl.ds(*self.rows[half])]

        def copy(self, kind, i, piece, part=0):
            device = at(dx=i) if kind in (0, 3) else at(dz=i)
            ss, rs = pg_ss.at[self.number, kind, i - 1, part], pg_rs.at[self.number, kind, i - 1]
            return send(piece, piece, ss, rs, device)

        def phase1(self):
            self.one = {}
            for i in (2, 1, 3):
                for half in range(2):
                    self.one[half, i] = go(lambda half=half, i=i: self.copy(half, i, self.tile(half)))

        def phase2(self):
            for half, i in self.one:
                self.one[half, i]().wait_recv()
            for i in (2, 1, 3):
                for half in range(2):
                    go(lambda half=half, i=i: self.copy(2 + half, i, self.line(half)))

        def own(self):
            self.phase1()
            for i in (2, 1, 3):
                for half in range(2):
                    go(lambda half=half, i=i: self.copy(2 + half, i, self.tile(half)))

        def forward(self):
            for k, i in enumerate((1, 3, 2)):
                for half in range(2):
                    self.one[half, i]().wait_recv()
                    back = {"dx": 4 - i} if half == 0 else {"dz": 4 - i}
                    for to in (2, 1, 3):
                        go(
                            lambda half=half, to=to, back=back, k=k: self.copy(
                                2 + half, to, self.tile(half, **back), 1 + k
                            )
                        )

        def done(self, halves=(0, 1), peers=(1, 3, 2)):
            for half in halves:
                for i in peers:
                    self.copy(2 + half, i, self.line(half)).wait_recv()

    def slice_of(d):
        return lax.rem(y + d, 4) * 2 + core

    def y_tiles(t):
        copies = {}
        for e in (2, 1, 3):
            rows = 128 if e == 2 else NEAR[t]
            if not rows:
                continue

            def make(e=e, rows=rows):
                piece = ybuf.at[t, row, z, x, pl.ds(0, rows)]
                return send(piece, piece, yt_ss.at[t, e - 1], yt_rs.at[t, e - 1], at(dy=e))

            copies[e] = go(make)
        return copies

    def y_line(t, back):
        for e in (1, 3):

            def make(e=e):
                piece = ybuf.at[t, row, :, lax.rem(x + 4 - back, 4), pl.ds(64, 64)]
                return send(piece, piece, yd_ss.at[t, e // 2, back], yd_rs.at[t, e // 2], at(dy=e))

            go(make)

    def y_line_wait(t, e):
        piece = ybuf.at[t, row, :, :, pl.ds(64, 64)]
        send(piece, piece, yd_ss.at[t, e // 2, 0], yd_rs.at[t, e // 2], at(dy=e)).wait_recv()

    def y_rest(t):
        copies = {}
        if NEAR[t] < 64:
            for e in (1, 3):

                def make(e=e):
                    piece = ybuf.at[t, row, :, :, pl.ds(NEAR[t], 64 - NEAR[t])]
                    return send(piece, piece, yr_ss.at[t, e // 2], yr_rs.at[t, e // 2], at(dy=e))

                copies[e] = go(make)
        return copies

    def across_copy(t, d, h):
        piece = ybuf.at[t, slice_of(d), :, :, pl.ds(64 * h, 64)]
        return send(piece, piece, cc_ss.at[t, d, h], cc_rs.at[t, d, h], at(other=True))

    def across(t, d, h):
        go(lambda: across_copy(t, d, h))

    def crossed(t, d, h):
        across_copy(t, d, h).wait_recv()

    def own_lines(t, gather, peers):
        for i in peers:
            gather.done((1,), (i,))
            y_line(t, i)

    own = [Gather(2 + t, ybuf.at[t, row], 0, 128) for t in range(2)]
    far = [
        {
            d: Gather(4 + 3 * t + d - 1, ybuf.at[t, slice_of(d)], 0, 128 if d == 2 else NEAR[t])
            for d in (2, 1, 3)
            if d == 2 or NEAR[t]
        }
        for t in range(2)
    ]
    g_b, g_f = Gather(0, b0, 0, 128), Gather(1, b1, 0, 128)

    def arrived(t, d, h):
        if d == 2:
            far[t][2].done((h,))
        elif h == 1:
            y_line_wait(t, 4 - d)
        else:
            if d in far[t]:
                far[t][d].done()
            if NEAR[t] < 64:
                rest[t][4 - d]().wait_recv()
        across(t, d, h)

    d_load.wait()
    b0_send(0).wait_recv()
    g_b.own()
    g_b.forward()
    d0 = split(dbuf[0])
    g_b.done()
    ybuf[0, row, z, x] = dot3(d0, split(b0[...].reshape(2048, 128)))
    own[0].own()
    tiles0 = y_tiles(0)

    half = l10.at[core]
    l10_on = send(half, half, l_ss.at[1, 1], l_rs.at[core], (4 + core, col))
    l10_across = send(half, half, l_ss.at[1, 0], l_rs.at[core], at(other=True))
    first = jnp.logical_or(row == 2, row == 7)

    @pl.when(first)
    def _():
        l10_on.wait_recv()
        l10_on.start()
        l10_across.start()

    own[0].forward()
    y_line(0, 0)

    @pl.when(jnp.logical_and(y > 0, jnp.logical_not(first)))
    def _():
        l10_across.wait_recv()
        l10_across.start()

    @pl.when(y > 0)
    def _():
        send(half, l10.at[1 - core], l_ss.at[1, 0], l_rs.at[1 - core], at(other=True)).wait_recv()

    @pl.when(y == 0)
    def _():
        for h in range(2):
            send(l10.at[h], l10.at[h], l_ss.at[1, 0], l_rs.at[h], at(other=True)).wait_recv()

    send(b1_tile, b1_tile, s_ss.at[0], s_rs.at[1], (row, col)).wait_recv()
    lower = [split(l10[h]) for h in range(2)]
    own_lines(0, own[0], (1, 3))
    own_lines(0, own[0], (2,))
    own[0].done((0,))

    mine = ybuf[0, row].reshape(2048, 128)
    b1[z, x] = b1_tile[...] - (dot3(lower[0], split(mine[:1024])) + dot3(lower[1], split(mine[1024:])))
    g_f.own()
    across(0, 0, 0)
    across(0, 0, 1)
    rest = [y_rest(0), {}]
    tiles0[2]().wait_recv()
    far[0][2].own()
    g_f.forward()
    far[0][2].forward()
    out_load.wait()

    def solve_second():
        arrived(0, 1, 1)
        arrived(0, 3, 1)
        d1 = split(dbuf[1])
        g_f.done()
        ybuf[1, row, z, x] = dot3(d1, split(b1[...].reshape(2048, 128)))
        own[1].own()
        second_tiles.update(y_tiles(1))
        crossed(0, 1, 1)

    second_tiles = {}

    def start_far():
        own[1].forward()
        y_line(1, 0)
        second_tiles[2]().wait_recv()
        far[1][2].own()
        for d in (1, 3):
            second_tiles[4 - d]().wait_recv()
            far[1][d].phase1()
        arrived(0, 2, 0)
        arrived(0, 2, 1)
        crossed(0, 2, 0)

    def forward_far():
        own_lines(1, own[1], (1, 3))
        far[1][2].forward()
        crossed(0, 2, 1)

    def second_gathered():
        own_lines(1, own[1], (2,))
        own[1].done((0,))
        across(1, 0, 0)
        across(1, 0, 1)
        far[1][1].phase2()
        far[1][3].phase2()
        arrived(0, 1, 0)
        arrived(0, 3, 0)
        crossed(0, 1, 0)

    def opposite():
        arrived(1, 2, 0)
        arrived(1, 2, 1)
        crossed(1, 0, 1)

    def near_high():
        arrived(1, 1, 1)
        arrived(1, 3, 1)
        crossed(1, 2, 1)

    def near_low():
        arrived(1, 1, 0)
        arrived(1, 3, 0)
        crossed(1, 1, 1)

    order = [(0, 0, 0), (0, 0, 1), (0, 1, 1), (0, 3, 1), (0, 2, 0), (0, 2, 1), (0, 1, 0), (0, 3, 0)]
    order += [(1, 0, 0), (1, 0, 1), (1, 2, 0), (1, 2, 1), (1, 1, 1), (1, 3, 1), (1, 1, 0), (1, 3, 0)]
    controls = {
        (0, 1, 1): solve_second,
        (0, 2, 0): start_far,
        (0, 2, 1): forward_far,
        (0, 1, 0): second_gathered,
        (1, 0, 1): opposite,
        (1, 2, 1): near_high,
        (1, 1, 1): near_low,
    }

    def job(k, carry):
        for i, unit in enumerate(order):
            pl.when(k == i)(controls.get(unit, lambda unit=unit: crossed(*unit)))

        def of(place):
            return sum((k == i).astype(jnp.int32) * unit[place] for i, unit in enumerate(order) if unit[place])

        t, d, h = of(0), of(1), of(2)
        q = lax.rem(y + d, 4)
        columns = pl.ds(pl.multiple_of(256 * q, 256), 256)
        for c in range(2):
            rows = ybuf[t, 2 * q + c, :, :, pl.ds(pl.multiple_of(64 * h, 64), 64), :]
            high, low = split(rows.reshape(1024, 128))
            yhi[:, 128 * c : 128 * c + 128] = high
            ylo[:, 128 * c : 128 * c + 128] = low
        out[:, columns] -= dot3((lhi[t, h], llo[t, h]), (yhi[...], ylo[...]))

        return carry

    lax.fori_loop(0, 16, job, 0)

    @pl.when(row < 2)
    def _():
        for r in range(8):
            out[0:128, 128 * r : 128 * r + 128] = ybuf[row, r, z, x]

    for make in sent:
        make().wait_send()

    @pl.when(row == 0)
    def _():
        for r in range(1, 8):
            b0_send(r).wait_send()

    @pl.when(row == 1)
    def _():
        for r in (0, 2, 3, 4, 5, 6, 7):
            b1_send(r).wait_send()
        for r, h in l10_parts:
            l10_send(r, h).wait_send()

    @pl.when(y > 0)
    def _():
        l10_across.wait_send()

    @pl.when(first)
    def _():
        l10_on.wait_send()


def on_device(lower_panel, test_cross, diag_inverse):
    V = pltpu.VMEM
    out = pl.pallas_call(
        kernel,
        out_shape=pltpu.VMEM((896, 1024), F32),
        in_specs=[pl.BlockSpec(memory_space=pl.ANY)] * 3,
        out_specs=pl.BlockSpec(memory_space=pltpu.VMEM),
        scratch_shapes=[
            V((2, 2, 896, 1024), BF16),
            V((2, 2, 896, 1024), BF16),
            V((2, 128, 4096), F32),
            V((2, 128, 2048), F32),
            V((2, 128, 1024), F32),
            V((4, 4, 128, 128), F32),
            V((4, 4, 128, 128), F32),
            V((128, 128), F32),
            V((2, 8, 4, 4, 128, 128), F32),
            V((1024, 256), BF16),
            V((1024, 256), BF16),
            DMA((2,)), DMA((2,)),
            DMA((8,)), DMA((2,)), DMA((8, 2)), DMA((2,)),
            DMA((10, 4, 3, 4)), DMA((10, 4, 3)),
            DMA((2, 3)), DMA((2, 3)), DMA((2, 2, 4)), DMA((2, 2)), DMA((2, 2)), DMA((2, 2)),
            DMA((2, 4, 2)), DMA((2, 4, 2)),
        ],
        compiler_params=pltpu.CompilerParams(
            collective_id=0, has_side_effects=True, vmem_limit_bytes=54 * 2**20
        ),
        cost_estimate=pl.CostEstimate(flops=22 * 10**9, bytes_accessed=24 * 10**6, transcendentals=0),
    )(lower_panel, test_cross.reshape(896, 1024), diag_inverse)
    return out.reshape(test_cross.shape)


def solution(mesh):
    placed = (P(None, "row", "col", None), P(None, "row", "col", None), P(None, "col", None))
    return jax.shard_map(
        on_device,
        mesh=mesh,
        in_specs=placed,
        out_specs=P(None, "row", "col", None),
        check_vma=False,
    )
```

time: 123 us -> 101 us (0.82)
  the two profiles are of different devices: /device:TPU:16 before, /device:TPU:1 now
where the time goes in v2:
time: 101 us
  Pallas kernels  99.1 us (98%)
  local copies, waits for them, and re-layouts  1.84 us (2%)
    pallas_call x1, Pallas kernels, on_device(): pl.pallas_call(kernel, out_shape=pltpu.VMEM((896, 1024), F32), in_specs=[...  99.1 us

profile of v2, /device:TPU:1, one launch (start us, length us, event | category | flops | bytes accessed | tf_op | source)
XLA Modules:
  0.0 101.0 jit_solution(15780003070062528082)
XLA Ops:
  0.0 99.1 %shard_map.37 = f32[896,1024]{1,0:T(8,128)S(1)} custom-call(f32[7,1,128,4096]{3,2,1,0:T(8,128)} %panel.1, f32[896,1024]{1,0:T(8,128)} %bitcast.5, f32[2,128,2048]{2,1,0:T(8,128)} %diag.1), custom_call_target="tpu_custom_call" | custom-call | flops 22000001024 | bytes 24000000 | tf_op jit(solution)/shard_map/pallas_call | solution.py:449
  99.1 1.8 %copy.6 = f32[7,1,128,1024]{3,2,1,0:T(8,128)} copy(f32[7,1,128,1024]{3,2,1,0:T(8,128)S(1)} %bitcast.4) | data formatting | bytes 7340032

commit v3 on v2

--- a/solution.py
+++ b/solution.py
@@ -123,13 +123,11 @@
 
     @pl.when(row == 1)
     def _():
-        for r, h in l10_parts[:4]:
+        for r, h in l10_parts[:2]:
             l10_send(r, h).start()
         for r in (4, 5, 2, 3, 6, 7, 0):
             b1_send(r).start()
         pltpu.make_async_copy(tile_of(1), b1_tile, s_rs.at[1]).start()
-        for r, h in l10_parts[4:]:
-            l10_send(r, h).start()
         for h in range(2):
             pltpu.make_async_copy(l10_half(h), l10.at[h], l_rs.at[h]).start()
 
@@ -275,26 +273,36 @@
     b0_send(0).wait_recv()
     g_b.own()
     g_b.forward()
+
+    @pl.when(row == 1)
+    def _():
+        for r, h in l10_parts[:2]:
+            l10_send(r, h).wait_send()
+        for r, h in l10_parts[2:]:
+            l10_send(r, h).start()
+
     d0 = split(dbuf[0])
+
+    half = l10.at[core]
+    l10_on = send(half, half, l_ss.at[1, 1], l_rs.at[core], (4 + core, col))
+    l10_across = send(half, half, l_ss.at[1, 0], l_rs.at[core], at(other=True))
+    first = jnp.logical_or(row == 2, row == 7)
+
+    @pl.when(first)
+    def _():
+        l10_on.wait_recv()
+        l10_on.start()
+        l10_across.start()
+
     g_b.done()
     ybuf[0, row, z, x] = dot3(d0, split(b0[...].reshape(2048, 128)))
     own[0].own()
     tiles0 = y_tiles(0)
 
-    half = l10.at[core]
-    l10_on = send(half, half, l_ss.at[1, 1], l_rs.at[core], (4 + core, col))
-    l10_across = send(half, half, l_ss.at[1, 0], l_rs.at[core], at(other=True))
-    first = jnp.logical_or(row == 2, row == 7)
-
-    @pl.when(first)
-    def _():
-        l10_on.wait_recv()
-        l10_on.start()
-        l10_across.start()
-
     own[0].forward()
     y_line(0, 0)
 
+    own_lines(0, own[0], (1, 3))
     @pl.when(jnp.logical_and(y > 0, jnp.logical_not(first)))
     def _():
         l10_across.wait_recv()
@@ -311,7 +319,6 @@
 
     send(b1_tile, b1_tile, s_ss.at[0], s_rs.at[1], (row, col)).wait_recv()
     lower = [split(l10[h]) for h in range(2)]
-    own_lines(0, own[0], (1, 3))
     own_lines(0, own[0], (2,))
     own[0].done((0,))
 
@@ -432,7 +439,7 @@
     def _():
         for r in (0, 2, 3, 4, 5, 6, 7):
             b1_send(r).wait_send()
-        for r, h in l10_parts:
+        for r, h in l10_parts[2:]:
             l10_send(r, h).wait_send()
 
     @pl.when(y > 0)

time: 101 us -> 95.5 us (0.946)
  Pallas kernels: 99.1 us -> 93.4 us
    pallas_call x1, Pallas kernels: 99.1 us -> 93.4 us  [on_device(): pl.pallas_call(kernel, out_shape=pltpu.VMEM((896, 1024), F32), in_specs=[...]
where the time goes in v3:
time: 95.5 us; the launch traced here: 95.3 us
  Pallas kernels  93.4 us (98%)
  local copies, waits for them, and re-layouts  1.84 us (2%)
    pallas_call x1, Pallas kernels, on_device(): pl.pallas_call(kernel, out_shape=pltpu.VMEM((896, 1024), F32), in_specs=[...  93.4 us

profile of v3, /device:TPU:1, one launch (start us, length us, event | category | flops | bytes accessed | tf_op | source)
XLA Modules:
  0.0 95.3 jit_solution(10678465943506454656)
XLA Ops:
  0.0 93.4 %shard_map.37 = f32[896,1024]{1,0:T(8,128)S(1)} custom-call(f32[7,1,128,4096]{3,2,1,0:T(8,128)} %panel.1, f32[896,1024]{1,0:T(8,128)} %bitcast.5, f32[2,128,2048]{2,1,0:T(8,128)} %diag.1), custom_call_target="tpu_custom_call" | custom-call | flops 22000001024 | bytes 24000000 | tf_op jit(solution)/shard_map/pallas_call | solution.py:456
  93.5 1.8 %copy.6 = f32[7,1,128,1024]{3,2,1,0:T(8,128)} copy(f32[7,1,128,1024]{3,2,1,0:T(8,128)S(1)} %bitcast.4) | data formatting | bytes 7340032

commit v4 on v3

--- a/solution.py
+++ b/solution.py
@@ -131,9 +131,6 @@
         for h in range(2):
             pltpu.make_async_copy(l10_half(h), l10.at[h], l_rs.at[h]).start()
 
-    for a in range(5, 7):
-        convert(a)
-
     class Gather:
         def __init__(self, number, view, lo, hi):
             self.number, self.view = number, view
@@ -281,6 +278,8 @@
         for r, h in l10_parts[2:]:
             l10_send(r, h).start()
 
+    for a in range(5, 7):
+        convert(a)
     d0 = split(dbuf[0])
 
     half = l10.at[core]
@@ -340,8 +339,8 @@
         d1 = split(dbuf[1])
         g_f.done()
         ybuf[1, row, z, x] = dot3(d1, split(b1[...].reshape(2048, 128)))
+        second_tiles.update(y_tiles(1))
         own[1].own()
-        second_tiles.update(y_tiles(1))
         crossed(0, 1, 1)
 
     second_tiles = {}

time: 95.5 us -> 92.9 us (0.973)
  Pallas kernels: 93.4 us -> 90.7 us
    pallas_call x1, Pallas kernels: 93.4 us -> 90.7 us  [on_device(): pl.pallas_call(kernel, out_shape=pltpu.VMEM((896, 1024), F32), in_specs=[...]
where the time goes in v4:
time: 92.9 us; the launch traced here: 92.5 us
  Pallas kernels  90.7 us (98%)
  local copies, waits for them, and re-layouts  1.84 us (2%)
    pallas_call x1, Pallas kernels, on_device(): pl.pallas_call(kernel, out_shape=pltpu.VMEM((896, 1024), F32), in_specs=[...  90.7 us

profile of v4, /device:TPU:1, one launch (start us, length us, event | category | flops | bytes accessed | tf_op | source)
XLA Modules:
  0.0 92.5 jit_solution(11035213728320510127)
XLA Ops:
  0.0 90.7 %shard_map.37 = f32[896,1024]{1,0:T(8,128)S(1)} custom-call(f32[7,1,128,4096]{3,2,1,0:T(8,128)} %panel.1, f32[896,1024]{1,0:T(8,128)} %bitcast.5, f32[2,128,2048]{2,1,0:T(8,128)} %diag.1), custom_call_target="tpu_custom_call" | custom-call | flops 22000001024 | bytes 24000000 | tf_op jit(solution)/shard_map/pallas_call | solution.py:455
  90.7 1.8 %copy.6 = f32[7,1,128,1024]{3,2,1,0:T(8,128)} copy(f32[7,1,128,1024]{3,2,1,0:T(8,128)S(1)} %bitcast.4) | data formatting | bytes 7340032

commit v5 on v4

--- a/solution.py
+++ b/solution.py
@@ -345,7 +345,11 @@
 
     second_tiles = {}
 
+    gone = []
+
     def start_far():
+        gone.extend(sent)
+        sent.clear()
         own[1].forward()
         y_line(1, 0)
         second_tiles[2]().wait_recv()
@@ -374,6 +378,8 @@
         crossed(0, 1, 0)
 
     def opposite():
+        for make in gone:
+            make().wait_send()
         arrived(1, 2, 0)
         arrived(1, 2, 1)
         crossed(1, 0, 1)

time: 92.9 us -> 92.7 us (level)
  no operation moved by 1% of the time
where the time goes in v5:
time: 92.7 us; the launch traced here: 92.4 us
  Pallas kernels  90.5 us (98%)
  local copies, waits for them, and re-layouts  1.84 us (2%)
    pallas_call x1, Pallas kernels, on_device(): pl.pallas_call(kernel, out_shape=pltpu.VMEM((896, 1024), F32), in_specs=[...  90.5 us

profile of v5, /device:TPU:1, one launch (start us, length us, event | category | flops | bytes accessed | tf_op | source)
XLA Modules:
  0.0 92.4 jit_solution(9165035603585127159)
XLA Ops:
  0.0 90.5 %shard_map.37 = f32[896,1024]{1,0:T(8,128)S(1)} custom-call(f32[7,1,128,4096]{3,2,1,0:T(8,128)} %panel.1, f32[896,1024]{1,0:T(8,128)} %bitcast.5, f32[2,128,2048]{2,1,0:T(8,128)} %diag.1), custom_call_target="tpu_custom_call" | custom-call | flops 22000001024 | bytes 24000000 | tf_op jit(solution)/shard_map/pallas_call | solution.py:461
  90.5 1.8 %copy.6 = f32[7,1,128,1024]{3,2,1,0:T(8,128)} copy(f32[7,1,128,1024]{3,2,1,0:T(8,128)S(1)} %bitcast.4) | data formatting | bytes 7340032
